TPU v7x, 32 devices: a whole 2x2x4 slice. The times are simulated.
32 devices in a mesh: group: 2 (over y), seq: 4 (over z), head: 4 (over x, core), pair: 1.
Axes of the slice: x: 2, y: 2, z: 4, core: 2. Of those that a mesh axis runs over, the one named last changes fastest.
Arguments:
- query_states: bfloat16 [2048, 4096], P(('group', 'seq'), ('head', 'pair')), parts along dimension 0, may hold values from -6 to 6
- key_states: bfloat16 [2048, 512], P(('group', 'seq'), 'head'), parts along dimension 0, may hold values from -6 to 6
- value_states: bfloat16 [2048, 512], P(('group', 'seq'), 'head'), parts along dimension 0, may hold values from -12 to 12
- sink_logits: float32 [64], P(('head', 'pair')), may hold values from 0 to 5
- segment_ids: int32 [2048], P('group'), parts along dimension 0, may hold values from 0 to 11, never falling along the last dimension, each value on 1 to 256 neighbouring positions
- residual: bfloat16 [2048, 1536], P(('group', 'seq', 'head', 'pair')), parts along dimension 0, may hold values from -6 to 6
- out_weight: bfloat16 [4096, 1536], P(('head', 'pair')), may hold values from -0.09375 to 0.09375
- norm_gain: float32 [1536], replicated, may hold values from 0.5 to 1.5
- expert_ids: int32 [2048, 4], P(('group', 'seq', 'head', 'pair')), parts along dimension 0, may hold values from 0 to 7, all different within a row; in each aligned block of 64 rows (0 to 63, 64 to 127, ...) at most 48 rows name the same one
- route_weights: float32 [2048, 4], P(('group', 'seq', 'head', 'pair')), parts along dimension 0, may hold values from 0.1 to 1
- gate_proj: bfloat16 [16, 1536, 768], P(('seq', 'head'), None, 'pair'), may hold values from -0.15625 to 0.15625
- up_proj: bfloat16 [16, 1536, 768], P(('seq', 'head'), None, 'pair'), may hold values from -0.15625 to 0.15625
- down_proj: bfloat16 [16, 768, 1536], P(('seq', 'head'), 'pair'), may hold values from -0.15625 to 0.15625
Outputs:
- layer_out: bfloat16 [2048, 1536], P(('group', 'seq', 'head', 'pair')), parts along dimension 0
There are 2 independent parts, one for each index of `group`. A program takes and returns all parts, laid end to end along the dimension named above; an argument that names none is the same for every part. Nothing has to cross between parts.
Inputs may be any that keep to these rules, and one draw needn't show every extreme that they name: `segment_ids`: never falling along the sequence; each passage holds 1 to 256 tokens and one holds exactly 256. `expert_ids`: each row names 4 different experts. Among the rows of one device (aligned blocks of 64 rows) no expert is named by more than 48 rows, a bound that some block reaches.
All inputs are finite; a program needn't handle non-finite values.
Results may differ from a plain program's by a relative error of at most 0.015.
Values may be sent and summed in bfloat16 or wider, within the bound.
A program may use at most 64 MiB of HBM per device.

v0:
```python
import jax
import jax.numpy as jnp
from jax import lax
from jax.sharding import PartitionSpec as P

HEADS = 64
KV_HEADS = 8
HEAD_DIM = 64
WINDOW = 128


def passed_along(value, axis, by):
    peers = lax.axis_size(axis)
    pairs = [(i, i + by) for i in range(peers) if 0 <= i + by < peers]
    return lax.ppermute(value, axis, pairs)


def partner(value, axis, distance):
    return lax.ppermute(value, axis, [(i, i ^ 1 << distance) for i in range(lax.axis_size(axis))])


def round_keep(values):
    return lax.optimization_barrier(values.astype(jnp.bfloat16)).astype(jnp.float32)


def window_attention(
    query_block, key_block, value_block, query_pos, key_pos, query_seg, key_seg, sink_logits
):
    scores = jnp.einsum(
        "qhd,khd->hqk", query_block, key_block, preferred_element_type=jnp.float32
    ) * HEAD_DIM ** (-0.5)
    visible = (key_pos[None, :] <= query_pos[:, None]) & (
        query_pos[:, None] - key_pos[None, :] < WINDOW
    )
    visible = visible & (key_pos[None, :] >= 0) & (key_seg[None, :] == query_seg[:, None])
    masked = jnp.where(visible[None], scores, -1e30)
    row_max = jnp.maximum(jnp.max(masked, -1), sink_logits[:, None])
    weights_exp = jnp.exp(masked - row_max[..., None])
    denominator = jnp.sum(weights_exp, -1) + jnp.exp(sink_logits[:, None] - row_max)
    probs = (weights_exp / denominator[..., None]).astype(jnp.bfloat16)
    attended = jnp.einsum("hqk,khd->qhd", probs, value_block, preferred_element_type=jnp.float32)
    return attended.astype(jnp.bfloat16)


def per_device(
    query_states,
    key_states,
    value_states,
    sink_logits,
    segment_ids,
    residual,
    out_weight,
    norm_gain,
    expert_ids,
    route_weights,
    gate_proj,
    up_proj,
    down_proj,
):
    tok_rows = query_states.shape[0]
    local_heads = query_states.shape[1] // HEAD_DIM
    local_groups = key_states.shape[1] // HEAD_DIM
    group_size = HEADS // KV_HEADS
    tail_keys, tail_values = passed_along(
        (key_states[tok_rows - WINDOW :], value_states[tok_rows - WINDOW :]), "seq", 1
    )
    ext_keys = jnp.concatenate([tail_keys, key_states], 0).reshape(
        tok_rows + WINDOW, local_groups, HEAD_DIM
    )
    ext_values = jnp.concatenate([tail_values, value_states], 0).reshape(
        tok_rows + WINDOW, local_groups, HEAD_DIM
    )
    kv_owner = (
        lax.axis_index("pair") * local_heads + jnp.arange(local_heads, dtype=jnp.int32)
    ) // group_size
    head_select = (kv_owner[:, None] == jnp.arange(local_groups, dtype=jnp.int32)[None, :]).astype(
        jnp.bfloat16
    )
    keys_per_head = jnp.einsum(
        "kcd,hc->khd", ext_keys, head_select, preferred_element_type=jnp.float32
    ).astype(jnp.bfloat16)
    values_per_head = jnp.einsum(
        "kcd,hc->khd", ext_values, head_select, preferred_element_type=jnp.float32
    ).astype(jnp.bfloat16)
    query_heads = query_states.reshape(tok_rows, local_heads, HEAD_DIM)
    seq_start = lax.axis_index("seq") * tok_rows
    seg_padded = jnp.concatenate([jnp.full((WINDOW,), -1, jnp.int32), segment_ids], 0)
    block_rows = min(512, tok_rows)

    def attend(block_index):
        first_row = block_index * block_rows
        query_pos = seq_start + first_row + jnp.arange(block_rows, dtype=jnp.int32)
        key_pos = seq_start + first_row - WINDOW + jnp.arange(block_rows + WINDOW, dtype=jnp.int32)
        query_seg = lax.dynamic_slice_in_dim(segment_ids, seq_start + first_row, block_rows, 0)
        key_seg = lax.dynamic_slice_in_dim(
            seg_padded, seq_start + first_row, block_rows + WINDOW, 0
        )
        return window_attention(
            query_heads,
            keys_per_head,
            values_per_head,
            query_pos,
            key_pos,
            query_seg,
            key_seg,
            sink_logits,
        )

    attended = lax.map(attend, jnp.arange(tok_rows // block_rows, dtype=jnp.int32))
    attended = attended.reshape(tok_rows, local_heads * HEAD_DIM)
    shard_rows = residual.shape[0]
    width = residual.shape[1]
    projected = lax.psum_scatter(
        round_keep(jnp.dot(attended, out_weight, preferred_element_type=jnp.float32)).astype(
            jnp.bfloat16
        ),
        ("head", "pair"),
        scatter_dimension=0,
        tiled=True,
    ).astype(jnp.float32)
    hidden_state = residual.astype(jnp.float32) + projected
    variance = jnp.mean(hidden_state * hidden_state, -1, keepdims=True)
    normed = (hidden_state * lax.rsqrt(variance + 1e-05) * norm_gain).astype(jnp.bfloat16)
    top_count = expert_ids.shape[1]
    experts = lax.axis_size("seq") * lax.axis_size("head") // 2
    capacity = min(shard_rows, max(2, 3 * shard_rows * top_count // (2 * experts)))
    flat_ids = expert_ids.reshape(-1)
    onehot = (flat_ids[:, None] == jnp.arange(experts, dtype=jnp.int32)[None, :]).astype(jnp.int32)
    before = jnp.cumsum(onehot, axis=0, dtype=jnp.int32) - onehot
    slot_rank = jnp.sum(before * onehot, -1)
    slot_index = flat_ids * capacity + slot_rank
    dispatch_mat = (
        slot_index[None, :] == jnp.arange(experts * capacity, dtype=jnp.int32)[:, None]
    ).astype(jnp.bfloat16)
    repeated = jnp.repeat(normed, top_count, axis=0)
    outgoing = jnp.dot(dispatch_mat, repeated, preferred_element_type=jnp.float32).astype(
        jnp.bfloat16
    )
    outgoing = outgoing.reshape(experts, capacity, width)
    half_idx = lax.axis_index("head") % 2
    half_width = width // 2
    split_rows = outgoing.reshape(experts, capacity, 2, half_width).transpose(0, 2, 1, 3)
    split_rows = split_rows.reshape(2 * experts, capacity, half_width)
    own_half = lax.all_to_all(split_rows, ("seq", "head"), split_axis=0, concat_axis=0, tiled=True)
    other_half = partner(own_half, "head", 0)
    arrived = jnp.where(
        half_idx == 0,
        jnp.concatenate([own_half, other_half], -1),
        jnp.concatenate([other_half, own_half], -1),
    )
    gate_local = gate_proj[0]
    up_local = up_proj[0]
    down_local = down_proj[0]
    piece_rows = lax.all_gather(arrived, "pair", axis=0, tiled=True)
    flat_rows = piece_rows.reshape(-1, width)
    gate_val = jnp.minimum(jnp.dot(flat_rows, gate_local, preferred_element_type=jnp.float32), 7.0)
    up_val = jnp.clip(jnp.dot(flat_rows, up_local, preferred_element_type=jnp.float32), -7.0, 7.0)
    activated = ((up_val + 1.0) * gate_val * jax.nn.sigmoid(1.702 * gate_val)).astype(jnp.bfloat16)
    partial_value = round_keep(jnp.dot(activated, down_local, preferred_element_type=jnp.float32))
    quarter_terms = partial_value.reshape(piece_rows.shape)
    pair_sums = lax.psum_scatter(
        quarter_terms.astype(jnp.bfloat16), "pair", scatter_dimension=0, tiled=True
    ).astype(jnp.float32)
    kept_half = lax.dynamic_slice_in_dim(pair_sums, half_idx * half_width, half_width, 2)
    given_half = lax.dynamic_slice_in_dim(pair_sums, (1 - half_idx) * half_width, half_width, 2)
    partner_half = partner(given_half.astype(jnp.bfloat16), "head", 0).astype(given_half.dtype)
    merged = kept_half + partner_half
    returned = lax.all_to_all(
        merged.astype(jnp.bfloat16), ("seq", "head"), split_axis=0, concat_axis=0, tiled=True
    ).astype(merged.dtype)
    expert_out = (
        returned.reshape(experts, 2, capacity, half_width)
        .transpose(0, 2, 1, 3)
        .reshape(experts, capacity, width)
    )
    slot_table = slot_index.reshape(shard_rows, top_count)
    columns_all = jnp.arange(experts * capacity, dtype=jnp.int32)
    combine_mat = jnp.sum(
        jnp.where(
            slot_table[:, :, None] == columns_all[None, None, :], route_weights[:, :, None], 0.0
        ),
        axis=1,
    )
    mixture = jnp.dot(
        combine_mat, expert_out.reshape(experts * capacity, width), precision=lax.Precision.HIGHEST
    )
    return (hidden_state + mixture).astype(jnp.bfloat16)


def solution(mesh):
    in_specs = (
        P(("group", "seq"), ("head", "pair")),
        P(("group", "seq"), "head"),
        P(("group", "seq"), "head"),
        P(("head", "pair")),
        P("group"),
        P(("group", "seq", "head", "pair"), None),
        P(("head", "pair"), None),
        P(),
        P(("group", "seq", "head", "pair"), None),
        P(("group", "seq", "head", "pair"), None),
        P(("seq", "head"), None, "pair"),
        P(("seq", "head"), None, "pair"),
        P(("seq", "head"), "pair", None),
    )
    out_specs = P(("group", "seq", "head", "pair"), None)
    return jax.shard_map(
        per_device, mesh=mesh, in_specs=in_specs, out_specs=out_specs, check_vma=False
    )
```

profile of v0, /device:TPU:0, one launch (start us, length us, event | category | flops | bytes accessed | tf_op | source)
XLA Modules:
  0.0 172.3 jit_solution(3354271913761056211)
XLA Ops:
  6.5 0.0 copy-start
  6.5 0.0 reduce-scatter.2.cloned.1.call-start
  6.5 1.1 copy.67
  7.6 4.9 %collective-permute-start.1 = (bf16[128,128]{0,1:T(8,128)(2,1)S(1)}, bf16[128,128]{0,1:T(8,128)(2,1)S(1)}, u32[]{:S(2)}, u32[]{:S(2)}) collective-permute-start(bf16[128,128]{0,1:T(8,128)(2,1)S(1)} %slice.17), channel_id=1, source_target_pairs={{0,4},{4,8},{8,12},{1,5},{5,9},{9,13},{2,6},{6,10},{10,14},{3,7},{... | collective-permute-start | bytes 98312 | tf_op jit(solution)/shard_map/ppermute | solution.py:15
  12.6 0.9 copy.64
  13.5 3.5 %collective-permute-start = (bf16[128,128]{0,1:T(8,128)(2,1)S(1)}, bf16[128,128]{0,1:T(8,128)(2,1)S(1)}, u32[]{:S(2)}, u32[]{:S(2)}) collective-permute-start(bf16[128,128]{0,1:T(8,128)(2,1)S(1)} %slice.16), channel_id=1, source_target_pairs={{0,4},{4,8},{8,12},{1,5},{5,9},{9,13},{2,6},{6,10},{10,14},{3,7},{... | collective-permute-start | bytes 98312 | tf_op jit(solution)/shard_map/ppermute | solution.py:15
  17.1 0.8 pad_dynamic-slice_fusion
  17.8 0.8 dynamic_slice.18
  18.6 0.2 fusion.21
  18.8 2.0 %copy.70 = bf16[256,1024]{0,1:T(8,128)(2,1)} copy(bf16[256,1024]{1,0:T(8,128)(2,1)} %param.13) | data formatting | bytes 1048576 | tf_op args[0]
  20.9 0.0 collective-permute-done.1
  20.9 0.5 fusion.13
  21.4 0.0 copy-start.6
  21.4 2.2 %fusion.1 = (f32[16,256]{1,0:T(8,128)S(1)}, f32[16,384,256]{2,1,0:T(8,128)S(1)}) fusion(pred[256,384]{0,1:T(8,128)(4,1)S(1)} %fusion.21, bf16[256,16,64]{0,2,1:T(8,128)(2,1)} %bitcast.70, bf16[384,16,64]{0,1,2:T(8,128)(2,1)S(1)} %fusion.13), kind=kOutput, calls=%fused_computation.4 | convolution fusion | flops 206041088 | bytes 7716864 | tf_op jit(solution)/shard_map/while/body/eval_jaxpr/qhd,khd->hqk/dot_general | solution.py:29
  23.6 0.0 copy-done.6
  23.6 0.1 broadcast_maximum_fusion
  23.7 1.3 fusion
  25.0 0.1 exponential_add_fusion
  25.0 0.0 collective-permute-done
  25.1 0.5 fusion.12
  25.5 1.8 %fusion.11 = bf16[16,64,256]{2,1,0:T(8,128)(2,1)S(1)} fusion(f32[16,384,256]{2,1,0:T(8,128)S(1)} %get-tuple-element.22, f32[16,256]{1,0:T(8,128)S(1)} %exponential_add_fusion, f32[16,256]{1,0:T(8,128)S(1)} %broadcast_maximum_fusion, pred[256,384]{0,1:T(8,128)(4,1)S(1)} %fusion.21, bf16[384,16,64]{0,1,2:T(8,128)(2,1)S(1)} %fusion.12), kind=kOutput, calls=%fused_computation.22 | convolution fusion | flops 209453056 | bytes 7733248 | tf_op jit(solution)/shard_map/while/body/eval_jaxpr/hqk,khd->qhd/dot_general | solution.py:41
  27.3 0.0 copy-done
  27.3 0.0 copy-start.5
  27.4 0.0 copy-start.2
  27.4 0.0 copy-start.4
  27.4 1.9 %convolution_convert_fusion.2 = bf16[256,1536]{1,0:T(8,128)(2,1)} fusion(bf16[256,1024]{0,1:T(8,128)(2,1)S(1)} %bitcast.73, bf16[1024,1536]{1,0:T(8,128)(2,1)S(1)} %copy-done), kind=kOutput, calls=%fused_computation.8 | convolution fusion | flops 805699584 | bytes 4456448 | tf_op jit(solution)/shard_map/dot_general | solution.py:114
  29.3 0.0 reduce-scatter.2.cloned.1.call-update
  29.3 0.0 copy-done.5
  29.3 0.1 copy.74
  29.4 0.1 eq.109
  29.5 0.1 eq.105
  29.6 0.6 reduce-window.6
  30.2 0.2 slice_reduce_fusion
  30.5 0.1 fusion.26
  30.6 21.3 %reduce-scatter.2.cloned.1.call-done = bf16[64,1536]{1,0:T(8,128)(2,1)} async-done(((bf16[256,1536]{1,0:T(8,128)(2,1)}), bf16[64,1536]{1,0:T(8,128)(2,1)}) %reduce-scatter.2.cloned.1.call-update) | async-done | bytes 196624 | tf_op jit(solution)/shard_map/reduce_scatter | solution.py:113
  51.9 0.0 copy-done.2
  51.9 1.1 multiply_reduce_fusion
  53.0 1.0 multiply_convert_fusion.1
  54.1 1.1 broadcast_in_dim.69
  55.1 2.3 %reshape.253 = bf16[256,1536]{1,0:T(8,128)(2,1)} reshape(bf16[64,4,1536]{2,1,0:T(4,128)(2,1)} %broadcast_in_dim.69) | data formatting | bytes 1572864 | tf_op jit(solution)/shard_map/reshape | solution.py:135
  57.4 2.6 %convolution_convert_fusion.1 = bf16[384,1536]{1,0:T(8,128)(2,1)} fusion(bf16[256,1536]{1,0:T(8,128)(2,1)} %reshape.253, s32[256]{0:T(256)S(1)} %multiply_add_fusion.1), kind=kOutput, calls=%fused_computation.7 | convolution fusion | flops 302678016 | bytes 1967104 | tf_op jit(solution)/shard_map/dot_general | solution.py:136
  60.1 3.7 %reshape_reshape.6 = bf16[8,48,2,768]{3,2,1,0:T(2,128)(2,1)} reshape(bf16[384,1536]{1,0:T(8,128)(2,1)} %convolution_convert_fusion.1) | data formatting | bytes 2359296 | tf_op jit(solution)/shard_map/reshape;reshape | solution.py:142
  63.7 1.4 copy.77
  65.2 34.1 %all_to_all.10 = bf16[16,48,768]{2,1,0:T(8,128)(2,1)} all-to-all(bf16[16,48,768]{2,1,0:T(8,128)(2,1)S(1)} %bitcast.67), channel_id=1, replica_groups=mesh['group'=2,'seq'=4,'head'=4,'pair'=1] {'seq','head'}, dimensions={0} | all-to-all | bytes 2359296 | tf_op jit(solution)/shard_map/all_to_all | solution.py:144
  99.2 0.3 collective-permute-start.2
  99.6 2.9 %collective-permute-done.2 = bf16[16,48,768]{2,1,0:T(8,128)(2,1)} collective-permute-done((bf16[16,48,768]{2,1,0:T(8,128)(2,1)}, bf16[16,48,768]{2,1,0:T(8,128)(2,1)}, u32[]{:S(2)}, u32[]{:S(2)}) %collective-permute-start.2) | collective-permute-done | bytes 1179680 | tf_op jit(solution)/shard_map/ppermute | solution.py:19
  102.4 6.6 %fusion.6 = f32[768,768]{1,0:T(8,128)} fusion(bf16[1,1536,768]{2,1,0:T(8,128)(2,1)} %param.24, bf16[768,768]{1,0:T(8,128)(2,1)} %bitcast.14, bf16[768,768]{1,0:T(8,128)(2,1)} %bitcast.13, pred[]{:T(512)S(6)} %eq.116), kind=kOutput, calls=%fused_computation.13 | convolution fusion | flops 1822556160 | bytes 7077889 | tf_op jit(solution)/shard_map/dot_general | solution.py:157
  109.0 10.8 %convolution_convert_fusion = bf16[768,1536]{1,0:T(8,128)(2,1)} fusion(bf16[1,768,1536]{2,1,0:T(8,128)(2,1)} %param.25, f32[768,768]{1,0:T(8,128)} %fusion.6, bf16[1,1536,768]{2,1,0:T(8,128)(2,1)} %param.23, bf16[768,768]{1,0:T(8,128)(2,1)} %bitcast.14, bf16[768,768]{1,0:T(8,128)(2,1)} %bitcast.13, pred[]{:T(512)S(6)} %eq.116), kind=kOutput, calls=%fused_computation.5 | convolution fusion | flops 3641573376 | bytes 11796481 | tf_op jit(solution)/shard_map/dot_general | solution.py:159
  119.8 2.3 %convert.1 = f32[16,48,1536]{2,1,0:T(8,128)S(1)} convert(bf16[16,48,1536]{2,1,0:T(8,128)(2,1)} %bitcast.69) | non-fusion elementwise | flops 1179648 | bytes 7077888 | tf_op jit(solution)/shard_map/convert_element_type | solution.py:163
  122.1 0.0 copy-start.1
  122.1 2.1 %copy-done.1 = f32[16,48,1536]{2,1,0:T(8,128)} copy-done((f32[16,48,1536]{2,1,0:T(8,128)}, f32[16,48,1536]{2,1,0:T(8,128)S(1)}, u32[]{:S(2)}) %copy-start.1) | copy-done | bytes 4718616
  124.2 1.2 dynamic-slice_convert_fusion
  125.4 0.3 collective-permute-start.3
  125.7 2.9 %collective-permute-done.3 = bf16[16,48,768]{2,1,0:T(8,128)(2,1)} collective-permute-done((bf16[16,48,768]{2,1,0:T(8,128)(2,1)}, bf16[16,48,768]{2,1,0:T(8,128)(2,1)}, u32[]{:S(2)}, u32[]{:S(2)}) %collective-permute-start.3) | collective-permute-done | bytes 1179680 | tf_op jit(solution)/shard_map/ppermute | solution.py:19
  128.6 3.3 %add_convert_fusion = bf16[16,48,768]{2,1,0:T(8,128)(2,1)} fusion(bf16[16,48,768]{2,1,0:T(8,128)(2,1)} %collective-permute-done.3, f32[16,48,1536]{2,1,0:T(8,128)} %copy-done.1, s32[]{:T(128)S(6)} %select_n.58), kind=kLoop, calls=%fused_computation.15 | loop fusion | flops 1769472 | bytes 4718596 | tf_op jit(solution)/shard_map/convert_element_type | solution.py:169
  131.9 4.5 %all-to-all-start.1 = ((bf16[16,48,768]{2,1,0:T(8,128)(2,1)}), bf16[16,48,768]{2,1,0:T(8,128)(2,1)}, u32[]{:S(2)}, u32[]{:S(2)}) async-start(bf16[16,48,768]{2,1,0:T(8,128)(2,1)} %add_convert_fusion), calls=%async_computation.2 | async-start | bytes 2359296 | tf_op jit(solution)/shard_map/all_to_all | solution.py:168
  136.5 0.1 reduce_sum.41
  136.6 0.1 copy.76
  136.6 0.0 copy-done.7
  136.7 0.1 select_reduce_fusion
  136.8 24.8 %all-to-all-done.1 = bf16[16,48,768]{2,1,0:T(8,128)(2,1)} async-done(((bf16[16,48,768]{2,1,0:T(8,128)(2,1)}), bf16[16,48,768]{2,1,0:T(8,128)(2,1)}, u32[]{:S(2)}, u32[]{:S(2)}) %all-to-all-start.1) | async-done | bytes 1179680 | tf_op jit(solution)/shard_map/all_to_all | solution.py:168
  161.6 2.3 %copy.78 = bf16[8,48,2,768]{3,2,1,0:T(2,128)(2,1)S(1)} copy(bf16[8,48,2,768]{3,1,2,0:T(8,128)(2,1)} %bitcast.21) | data formatting | bytes 2359296 | tf_op jit(solution)/shard_map/transpose | solution.py:173
  163.9 0.2 copy.80
  164.1 1.4 fusion.8
  (17 shorter events, 0.1 us)
Async XLA Ops:
  6.5 20.8 %copy-start = (bf16[1024,1536]{1,0:T(8,128)(2,1)S(1)}, bf16[1024,1536]{1,0:T(8,128)(2,1)}, u32[]{:S(2)}) copy-start(bf16[1024,1536]{1,0:T(8,128)(2,1)} %param.19) | copy-start | bytes 9437188
  6.5 45.4 %reduce-scatter.2.cloned.1.call-start = ((), (), s32[]{:S(2)}) async-start(), calls=%async_computation.3 | async-start | bytes 983040 | tf_op jit(solution)/shard_map/reduce_scatter | solution.py:113
  7.6 13.2 %collective-permute-start.1 = (bf16[128,128]{0,1:T(8,128)(2,1)S(1)}, bf16[128,128]{0,1:T(8,128)(2,1)S(1)}, u32[]{:S(2)}, u32[]{:S(2)}) collective-permute-start(bf16[128,128]{0,1:T(8,128)(2,1)S(1)} %slice.17), channel_id=1, source_target_pairs={{0,4},{4,8},{8,12},{1,5},{5,9},{9,13},{2,6},{6,10},{10,14},{3,7},{... | collective-permute-start | bytes 98312 | tf_op jit(solution)/shard_map/ppermute | solution.py:15
  13.5 11.5 %collective-permute-start = (bf16[128,128]{0,1:T(8,128)(2,1)S(1)}, bf16[128,128]{0,1:T(8,128)(2,1)S(1)}, u32[]{:S(2)}, u32[]{:S(2)}) collective-permute-start(bf16[128,128]{0,1:T(8,128)(2,1)S(1)} %slice.16), channel_id=1, source_target_pairs={{0,4},{4,8},{8,12},{1,5},{5,9},{9,13},{2,6},{6,10},{10,14},{3,7},{... | collective-permute-start | bytes 98312 | tf_op jit(solution)/shard_map/ppermute | solution.py:15
  21.4 2.2 %copy-start.6 = (f32[16]{0:T(128)S(1)}, f32[16]{0:T(128)}, u32[]{:S(2)}) copy-start(f32[16]{0:T(128)} %param.16) | copy-start | bytes 196
  27.3 1.9 %copy-start.5 = (s32[64,4]{0,1:T(4,128)S(1)}, s32[64,4]{0,1:T(4,128)}, u32[]{:S(2)}) copy-start(s32[64,4]{0,1:T(4,128)} %param.21) | copy-start | bytes 3076
  27.4 24.5 %copy-start.2 = (bf16[64,1536]{1,0:T(8,128)(2,1)S(1)}, bf16[64,1536]{1,0:T(8,128)(2,1)}, u32[]{:S(2)}) copy-start(bf16[64,1536]{1,0:T(8,128)(2,1)} %param.18) | copy-start | bytes 589828
  27.4 25.6 %copy-start.4 = (f32[1536]{0:T(1024)S(1)}, f32[1536]{0:T(1024)}, u32[]{:S(2)}) copy-start(f32[1536]{0:T(1024)} %param.20) | copy-start | bytes 18436
  99.2 3.2 %collective-permute-start.2 = (bf16[16,48,768]{2,1,0:T(8,128)(2,1)}, bf16[16,48,768]{2,1,0:T(8,128)(2,1)}, u32[]{:S(2)}, u32[]{:S(2)}) collective-permute-start(bf16[16,48,768]{2,1,0:T(8,128)(2,1)} %all_to_all.10), channel_id=1, source_target_pairs={{0,1},{1,0},{2,3},{3,2},{4,5},{5,4},{6,7},{7,6},{8,9},{9,8},{10,11... | collective-permute-start | bytes 3538952 | tf_op jit(solution)/shard_map/ppermute | solution.py:19
  122.1 2.1 %copy-start.1 = (f32[16,48,1536]{2,1,0:T(8,128)}, f32[16,48,1536]{2,1,0:T(8,128)S(1)}, u32[]{:S(2)}) copy-start(f32[16,48,1536]{2,1,0:T(8,128)S(1)} %convert.1) | copy-start | bytes 14155780
  125.4 3.2 %collective-permute-start.3 = (bf16[16,48,768]{2,1,0:T(8,128)(2,1)}, bf16[16,48,768]{2,1,0:T(8,128)(2,1)}, u32[]{:S(2)}, u32[]{:S(2)}) collective-permute-start(bf16[16,48,768]{2,1,0:T(8,128)(2,1)} %dynamic-slice_convert_fusion), channel_id=1, source_target_pairs={{0,1},{1,0},{2,3},{3,2},{4,5},{5,4},{6,7},{7,6},{8,9},{9,8},{10,11... | collective-permute-start | bytes 3538952 | tf_op jit(solution)/shard_map/ppermute | solution.py:19
  131.9 4.7 %copy-start.7 = (f32[64,4]{0,1:T(4,128)S(1)}, f32[64,4]{0,1:T(4,128)}, u32[]{:S(2)}) copy-start(f32[64,4]{0,1:T(4,128)} %param.22) | copy-start | bytes 3076
  131.9 29.6 %all-to-all-start.1 = ((bf16[16,48,768]{2,1,0:T(8,128)(2,1)}), bf16[16,48,768]{2,1,0:T(8,128)(2,1)}, u32[]{:S(2)}, u32[]{:S(2)}) async-start(bf16[16,48,768]{2,1,0:T(8,128)(2,1)} %add_convert_fusion), calls=%async_computation.2 | async-start | bytes 2359296 | tf_op jit(solution)/shard_map/all_to_all | solution.py:168
  161.6 2.5 %copy-start.3 = (bf16[64,1536]{1,0:T(8,128)(2,1)S(1)}, bf16[64,1536]{1,0:T(8,128)(2,1)}, u32[]{:S(2)}) copy-start(bf16[64,1536]{1,0:T(8,128)(2,1)} %reduce-scatter.2.cloned.1.call-done) | copy-start | bytes 589828
Sparse Core Ops, SparseCore 0:
  29.4 22.4 reduce-scatter.1
where the time goes:
time: 175 us; the launch traced here: 172 us
  waiting for transfers between devices  51.9 us (30%)
  blocking collectives  34.1 us (19%)
  matrix products  28.2 us (16%)
  local copies, waits for them, and re-layouts  19.8 us (11%)
  between operations  13.7 us (8%)
  starting transfers between devices  13.6 us (8%)
  other arithmetic  11.1 us (6%)
    all_to_all x1, blocking collectives, per_device(): lax.all_to_all(split_rows, ('seq', 'head'), split_axis=0, concat_axis=0,...  34.1 us
    all_to_all x1, waiting for transfers between devices, per_device(): lax.all_to_all(merged.astype(jnp.bfloat16), ('seq', 'head'), split_axis=0...  24.8 us
    reduce_scatter x1, waiting for transfers between devices, per_device(): lax.psum_scatter(round_keep(jnp.dot(attended, out_weight, preferred_eleme...  21.3 us
    dot_general x1, matrix products, per_device(): jnp.dot(activated, down_local, preferred_element_type=jnp.float32)  10.8 us
    ppermute x2, starting transfers between devices, passed_along(): return lax.ppermute(value, axis, pairs)  8.41 us
    dot_general x1, matrix products, per_device(): jnp.dot(flat_rows, up_local, preferred_element_type=jnp.float32)  6.56 us
    unnamed x21, local copies, waits for them, and re-layouts  6.48 us
    ppermute x2, waiting for transfers between devices, partner(): lax.ppermute(value, axis, [(i, i ^ 1 << distance) for i in range(lax.axis...  5.75 us
  transfers between devices with their start and end apart: 6, of which 4 were waited for; matrix products, arithmetic and copies ran while one was open for 6% of the time, Pallas kernels for 0%

commit v1 on v0

--- a/solution.py
+++ b/solution.py
@@ -1,6 +1,10 @@
+import functools
+
 import jax
 import jax.numpy as jnp
 from jax import lax
+from jax.experimental import pallas as pl
+from jax.experimental.pallas import tpu as pltpu
 from jax.sharding import PartitionSpec as P
 
 HEADS = 64
@@ -126,7 +130,11 @@
     capacity = min(shard_rows, max(2, 3 * shard_rows * top_count // (2 * experts)))
     flat_ids = expert_ids.reshape(-1)
     onehot = (flat_ids[:, None] == jnp.arange(experts, dtype=jnp.int32)[None, :]).astype(jnp.int32)
-    before = jnp.cumsum(onehot, axis=0, dtype=jnp.int32) - onehot
+    places = jnp.arange(flat_ids.shape[0], dtype=jnp.int32)
+    earlier = (places[None, :] < places[:, None]).astype(jnp.bfloat16)
+    before = jnp.dot(
+        earlier, onehot.astype(jnp.bfloat16), preferred_element_type=jnp.float32
+    ).astype(jnp.int32)
     slot_rank = jnp.sum(before * onehot, -1)
     slot_index = flat_ids * capacity + slot_rank
     dispatch_mat = (
@@ -187,6 +195,434 @@
     return (hidden_state + mixture).astype(jnp.bfloat16)
 
 
+BF16, F32 = jnp.bfloat16, jnp.float32
+MESH = pl.DeviceIdType.MESH
+LANES = 128
+
+
+def pick(table, index):
+    result = jnp.int32(table[0])
+    for i in range(1, len(table)):
+        result = jnp.where(index == i, jnp.int32(table[i]), result)
+    return result
+
+
+def as_column(row, dtype=F32):
+    n = row.shape[1]
+    at = lax.broadcasted_iota(jnp.int32, (n, n), 0) == lax.broadcasted_iota(jnp.int32, (n, n), 1)
+    return jnp.sum(jnp.where(at, row.astype(F32), 0.0), 1, keepdims=True)
+
+
+def layer_kernel(
+    planes, experts,
+    q_ref, k_ref, v_ref, sink_ref, seg_ref, res_ref, wo_hbm, gain_ref, ids_ref, rw_ref,
+    gate_hbm, up_hbm, down_hbm,
+    out_ref,
+    wo, gate, up, down, tail_k, tail_v, ext, kk, vv, attended, proj, proj_core, proj_x, proj_got,
+    hidden, xbuf, act, obuf, rc, s_out, rx, s_own, rz,
+    w_sem, halo_send, halo_recv, pc_send, pc_recv, px_send, px_recv,
+    gz_send, gz_recv, gx_send, gx_recv, gc_send, gc_recv,
+    rc_send, rc_recv, rx_send, rx_recv, rz_send, rz_recv,
+):
+    z, head = lax.axis_index("seq"), lax.axis_index("head")
+    x, core = head // 2, head % 2
+    other_core = {"seq": z, "head": x * 2 + 1 - core}
+    other_x = {"seq": z, "head": (1 - x) * 2 + core}
+    rows, width = res_ref.shape
+    ff = gate.shape[1]
+
+    def remote(src, dst, send, recv, to):
+        return pltpu.make_async_remote_copy(
+            src_ref=src, dst_ref=dst, send_sem=send, recv_sem=recv, device_id=to, device_id_type=MESH
+        )
+
+    loads = [
+        pltpu.make_async_copy(wo_hbm, wo, w_sem.at[0]),
+        pltpu.make_async_copy(gate_hbm.at[0], gate, w_sem.at[1]),
+        pltpu.make_async_copy(up_hbm.at[0], up, w_sem.at[2]),
+        pltpu.make_async_copy(down_hbm.at[0], down, w_sem.at[3]),
+    ]
+    for load in loads:
+        load.start()
+
+    barrier = pltpu.get_barrier_semaphore()
+    pl.semaphore_signal(barrier, inc=1, device_id=other_core, device_id_type=MESH)
+    pl.semaphore_signal(barrier, inc=1, device_id=other_x, device_id_type=MESH)
+    for far in range(1, planes):
+        to = {"seq": lax.rem(z + far, planes), "head": head}
+        pl.semaphore_signal(barrier, inc=1, device_id=to, device_id_type=MESH)
+    pl.semaphore_wait(barrier, planes + 1)
+
+    last = k_ref.shape[0] - WINDOW
+    after = {"seq": jnp.minimum(z + 1, planes - 1), "head": head}
+    halo = [
+        remote(k_ref.at[pl.ds(last, WINDOW)], tail_k, halo_send.at[0], halo_recv.at[0], after),
+        remote(v_ref.at[pl.ds(last, WINDOW)], tail_v, halo_send.at[1], halo_recv.at[1], after),
+    ]
+
+    @pl.when(z < planes - 1)
+    def _():
+        for copy in halo:
+            copy.start()
+
+    @pl.when(z == 0)
+    def _():
+        tail_k[...] = jnp.zeros_like(tail_k)
+        tail_v[...] = jnp.zeros_like(tail_v)
+
+    @pl.when(z > 0)
+    def _():
+        for copy in halo:
+            copy.wait_recv()
+
+    lane = lax.broadcasted_iota(jnp.int32, (1, LANES), 1)
+    low = lane < HEAD_DIM
+    for own, tail, to in ((k_ref, tail_k, kk), (v_ref, tail_v, vv)):
+        ext[0:WINDOW] = tail[...].astype(F32)
+        ext[WINDOW:] = own[...].astype(F32)
+        plain = ext[...]
+        turned = pltpu.roll(plain, HEAD_DIM, 1)
+        to[0, 0] = jnp.where(low, plain, 0.0).astype(BF16)
+        to[0, 1] = jnp.where(low, 0.0, turned).astype(BF16)
+        to[1, 0] = jnp.where(low, turned, 0.0).astype(BF16)
+        to[1, 1] = jnp.where(low, 0.0, plain).astype(BF16)
+
+    span = 2 * WINDOW
+    start = z * k_ref.shape[0]
+    heads = q_ref.shape[1] // HEAD_DIM
+    pairs_of_group = heads // 4
+
+    def attend(block):
+        first = pl.multiple_of(start + block * WINDOW, WINDOW)
+        row0 = pl.multiple_of(block * WINDOW, WINDOW)
+        prior = pl.multiple_of(jnp.maximum(first - WINDOW, 0), WINDOW)
+        seg_own = seg_ref[:, pl.ds(first, WINDOW)]
+        seg_prior = seg_ref[:, pl.ds(prior, WINDOW)]
+        seg_q = as_column(seg_own)
+        i = lax.broadcasted_iota(jnp.int32, (WINDOW, WINDOW), 0)
+        j = lax.broadcasted_iota(jnp.int32, (WINDOW, WINDOW), 1)
+        sees_prior = (j > i) & (seg_prior.astype(F32) == seg_q) & (first > 0)
+        sees_own = (j <= i) & (seg_own.astype(F32) == seg_q)
+
+        for group in range(2):
+            keys = jnp.concatenate(
+                [kk[group, 0, pl.ds(row0, span)], kk[group, 1, pl.ds(row0, span)]], 0
+            )
+            values = jnp.concatenate(
+                [vv[group, 0, pl.ds(row0, span)], vv[group, 1, pl.ds(row0, span)]], 0
+            )
+
+            def pair(at, _):
+                number = group * pairs_of_group + at
+                columns = pl.ds(pl.multiple_of(number * LANES, LANES), LANES)
+                scores = lax.dot_general(
+                    q_ref[pl.ds(row0, WINDOW), columns], keys, (((1,), (1,)), ((), ())),
+                    preferred_element_type=F32,
+                ) * HEAD_DIM ** (-0.5)
+                probs = []
+                for side in range(2):
+                    sink = sink_ref[number * 2 + side]
+                    far = jnp.where(sees_prior, scores[:, side * span : side * span + WINDOW], -1e30)
+                    near = jnp.where(
+                        sees_own, scores[:, side * span + WINDOW : (side + 1) * span], -1e30
+                    )
+                    top = jnp.maximum(jnp.max(jnp.maximum(far, near), 1, keepdims=True), sink)
+                    far, near = jnp.exp(far - top), jnp.exp(near - top)
+                    total = jnp.sum(far + near, 1, keepdims=True) + jnp.exp(sink - top)
+                    scale = 1.0 / total
+                    probs += [(far * scale).astype(BF16), (near * scale).astype(BF16)]
+                attended[pl.ds(row0, WINDOW), columns] = jnp.dot(
+                    jnp.concatenate(probs, 1), values, preferred_element_type=F32
+                ).astype(BF16)
+                return 0
+
+            lax.fori_loop(0, pairs_of_group, pair, 0)
+
+    mine_core = pl.ds(pl.multiple_of(core * rows, rows), rows)
+    its_core = pl.ds(pl.multiple_of((1 - core) * rows, rows), rows)
+    tile = 512 if width % 512 == 0 else LANES
+    to_core = []
+    for turn in range(2):
+        block = (1 - x) if turn == 0 else x
+        attend(block)
+        if turn == 0:
+            loads[0].wait()
+        row0 = pl.multiple_of(block * WINDOW, WINDOW)
+
+        def project(n, _):
+            columns = pl.ds(pl.multiple_of(n * tile, tile), tile)
+            proj[turn, :, columns] = jnp.dot(
+                attended[pl.ds(row0, WINDOW)], wo[:, columns], preferred_element_type=F32
+            ).astype(BF16)
+            return 0
+
+        lax.fori_loop(0, width // tile, project, 0)
+        copy = remote(
+            proj.at[turn, its_core], proj_core.at[turn], pc_send.at[turn], pc_recv.at[turn], other_core
+        )
+        copy.start()
+        to_core.append(copy)
+        if turn == 0:
+            copy.wait_recv()
+            proj_x[...] = (
+                proj[0, mine_core].astype(F32) + proj_core[0].astype(F32)
+            ).astype(BF16)
+            over_x = remote(proj_x, proj_got, px_send.at[0], px_recv.at[0], other_x)
+            over_x.start()
+
+    lanes = lax.broadcasted_iota(jnp.int32, (rows, LANES), 1)
+    weight = jnp.zeros((rows, LANES), F32)
+    for choice in range(ids_ref.shape[1]):
+        named = ids_ref[:, choice : choice + 1]
+        hit = (lanes == named) | (lanes == named + experts) | (lanes == named + 2 * experts)
+        weight += jnp.where(hit, rw_ref[:, choice : choice + 1], 0.0)
+    first_term = weight.astype(BF16).astype(F32)
+    second_term = (weight - first_term).astype(BF16).astype(F32)
+    third_term = weight - first_term - second_term
+    term = jnp.where(
+        lanes < experts, first_term, jnp.where(lanes < 2 * experts, second_term, third_term)
+    )
+
+    mine = pl.ds(pl.multiple_of((core * 2 + x) * rows, rows), rows)
+    its_x = pl.ds(pl.multiple_of((core * 2 + 1 - x) * rows, rows), rows)
+    both_mine = pl.ds(pl.multiple_of(core * 2 * rows, rows), 2 * rows)
+    both_other = pl.ds(pl.multiple_of((1 - core) * 2 * rows, rows), 2 * rows)
+
+    to_core[1].wait_recv()
+    over_x.wait_recv()
+    state = (
+        res_ref[...].astype(F32)
+        + proj[1, mine_core].astype(F32)
+        + proj_core[1].astype(F32)
+        + proj_got[...].astype(F32)
+    )
+    hidden[...] = state
+    variance = jnp.mean(state * state, -1, keepdims=True)
+    xbuf[z, mine, 0:width] = (state * lax.rsqrt(variance + 1e-05) * gain_ref[...]).astype(BF16)
+    xbuf[z, mine, width:] = term.astype(BF16)
+
+    orders = [
+        sorted(range(planes), key=lambda p, own=own: (abs(p - own), p)) for own in range(planes)
+    ]
+    order = [pick([orders[own][step] for own in range(planes)], z) for step in range(planes)]
+
+    def gather_z(step):
+        there = order[step]
+        part = xbuf.at[z, mine]
+        return remote(part, part, gz_send.at[step], gz_recv.at[z], {"seq": there, "head": head})
+
+    def gather_z_got(step):
+        part = xbuf.at[order[step], mine]
+        return remote(part, part, gz_send.at[step], gz_recv.at[order[step]], {"seq": order[step], "head": head})
+
+    def gather_x(step):
+        part = xbuf.at[order[step], mine]
+        return remote(part, part, gx_send.at[order[step]], gx_recv.at[order[step]], other_x)
+
+    def gather_x_got(step):
+        part = xbuf.at[order[step], its_x]
+        return remote(part, part, gx_send.at[order[step]], gx_recv.at[order[step]], other_x)
+
+    def gather_core(step):
+        part = xbuf.at[order[step], both_mine]
+        return remote(part, part, gc_send.at[order[step]], gc_recv.at[order[step]], other_core)
+
+    def gather_core_got(step):
+        part = xbuf.at[order[step], both_other]
+        return remote(part, part, gc_send.at[order[step]], gc_recv.at[order[step]], other_core)
+
+    def sum_core(step):
+        p = order[step]
+        return remote(obuf.at[p, both_other], rc.at[p], rc_send.at[p], rc_recv.at[p], other_core)
+
+    def sum_x(step):
+        p = order[step]
+        return remote(s_out.at[p], rx.at[p], rx_send.at[p], rx_recv.at[p], other_x)
+
+    def sum_z(step):
+        p = order[step]
+        return remote(s_own.at[p], rz.at[z], rz_send.at[p], rz_recv.at[z], {"seq": p, "head": head})
+
+    def sum_z_got(step):
+        p = order[step]
+        return remote(s_own.at[p], rz.at[p], rz_send.at[p], rz_recv.at[p], {"seq": p, "head": head})
+
+    its_x_part = pl.ds(pl.multiple_of((1 - x) * rows, rows), rows)
+    my_x_part = pl.ds(pl.multiple_of(x * rows, rows), rows)
+    at_core = pl.multiple_of(core * 2 * rows, rows)
+
+    def after_core(step):
+        p = order[step]
+        sum_core(step).wait_recv()
+        s_out[p] = (
+            obuf[p, pl.ds(pl.multiple_of(at_core + (1 - x) * rows, rows), rows)].astype(F32)
+            + rc[p, its_x_part].astype(F32)
+        ).astype(BF16)
+        sum_x(step).start()
+
+    def after_x(step):
+        p = order[step]
+        sum_x(step).wait_recv()
+        total = (
+            obuf[p, pl.ds(pl.multiple_of(at_core + x * rows, rows), rows)].astype(F32)
+            + rc[p, my_x_part].astype(F32)
+            + rx[p].astype(F32)
+        )
+        if step == 0:
+            hidden[...] += total
+        else:
+            s_own[p] = total.astype(BF16)
+            sum_z(step).start()
+
+    gather_x(0).start()
+    for step in range(1, planes):
+        gather_z(step).start()
+    gather_x_got(0).wait_recv()
+    gather_core(0).start()
+    for load in loads[1:]:
+        load.wait()
+    expert = (z * 4 + head) // 2
+    piece = 256 if ff % 256 == 0 else LANES
+
+    for step in range(planes):
+        p = order[step]
+        if step + 1 < planes:
+            gather_z_got(step + 1).wait_recv()
+            gather_x(step + 1).start()
+        gather_core_got(step).wait_recv()
+
+        def hidden_units(n, _):
+            columns = pl.ds(pl.multiple_of(n * piece, piece), piece)
+            normed = xbuf[p, :, 0:width]
+            g = jnp.minimum(jnp.dot(normed, gate[:, columns], preferred_element_type=F32), 7.0)
+            u = jnp.clip(jnp.dot(normed, up[:, columns], preferred_element_type=F32), -7.0, 7.0)
+            act[:, columns] = ((u + 1.0) * g * jax.nn.sigmoid(1.702 * g)).astype(BF16)
+            return 0
+
+        lax.fori_loop(0, ff // piece, hidden_units, 0)
+        if step >= 1:
+            after_core(step - 1)
+        if step + 1 < planes:
+            gather_x_got(step + 1).wait_recv()
+            gather_core(step + 1).start()
+        terms = xbuf[p, :, width:].astype(F32)
+        at = lax.broadcasted_iota(jnp.int32, terms.shape, 1)
+        hit = (at == expert) | (at == expert + experts) | (at == expert + 2 * experts)
+        share = jnp.sum(jnp.where(hit, terms, 0.0), 1, keepdims=True)
+
+        def outputs(n, _):
+            columns = pl.ds(pl.multiple_of(n * tile, tile), tile)
+            obuf[p, :, columns] = (
+                jnp.dot(act[...], down[:, columns], preferred_element_type=F32) * share
+            ).astype(BF16)
+            return 0
+
+        lax.fori_loop(0, width // tile, outputs, 0)
+        sum_core(step).start()
+        if step >= 1:
+            after_x(step - 1)
+    after_core(planes - 1)
+    after_x(planes - 1)
+    total = hidden[...]
+    for step in range(1, planes):
+        sum_z_got(step).wait_recv()
+        total += rz[order[step]].astype(F32)
+    out_ref[...] = total.astype(BF16)
+
+    @pl.when(z < planes - 1)
+    def _():
+        for copy in halo:
+            copy.wait_send()
+
+    for copy in to_core + [over_x]:
+        copy.wait_send()
+    for step in range(planes):
+        gather_x(step).wait_send()
+        gather_core(step).wait_send()
+        sum_core(step).wait_send()
+        sum_x(step).wait_send()
+        if step:
+            gather_z(step).wait_send()
+            sum_z(step).wait_send()
+
+
+def fused(
+    planes, query_states, key_states, value_states, sink_logits, segment_ids, residual, out_weight,
+    norm_gain, expert_ids, route_weights, gate_proj, up_proj, down_proj,
+):
+    rows, width = residual.shape
+    ff = gate_proj.shape[2]
+    plane = 4 * rows
+    tokens = query_states.shape[0]
+    vmem, hbm = pl.BlockSpec(memory_space=pltpu.VMEM), pl.BlockSpec(memory_space=pl.ANY)
+    smem = pl.BlockSpec(memory_space=pltpu.SMEM)
+    dma = pltpu.SemaphoreType.DMA
+    return pl.pallas_call(
+        functools.partial(layer_kernel, planes, gate_proj.shape[0] * planes * 4 // 2),
+        out_shape=jax.ShapeDtypeStruct((rows, width), BF16),
+        in_specs=[vmem, vmem, vmem, smem, vmem, vmem, hbm, vmem, vmem, vmem, hbm, hbm, hbm],
+        out_specs=vmem,
+        scratch_shapes=[
+            pltpu.VMEM(out_weight.shape, BF16),
+            pltpu.VMEM(gate_proj.shape[1:], BF16),
+            pltpu.VMEM(up_proj.shape[1:], BF16),
+            pltpu.VMEM(down_proj.shape[1:], BF16),
+            pltpu.VMEM((WINDOW, LANES), BF16),
+            pltpu.VMEM((WINDOW, LANES), BF16),
+            pltpu.VMEM((tokens + WINDOW, LANES), F32),
+            pltpu.VMEM((2, 2, tokens + WINDOW, LANES), BF16),
+            pltpu.VMEM((2, 2, tokens + WINDOW, LANES), BF16),
+            pltpu.VMEM(query_states.shape, BF16),
+            pltpu.VMEM((2, WINDOW, width), BF16),
+            pltpu.VMEM((2, rows, width), BF16),
+            pltpu.VMEM((rows, width), BF16),
+            pltpu.VMEM((rows, width), BF16),
+            pltpu.VMEM((rows, width), F32),
+            pltpu.VMEM((planes, plane, width + LANES), BF16),
+            pltpu.VMEM((plane, ff), BF16),
+            pltpu.VMEM((planes, plane, width), BF16),
+            pltpu.VMEM((planes, plane // 2, width), BF16),
+            pltpu.VMEM((planes, rows, width), BF16),
+            pltpu.VMEM((planes, rows, width), BF16),
+            pltpu.VMEM((planes, rows, width), BF16),
+            pltpu.VMEM((planes, rows, width), BF16),
+            dma((4,)),
+            *[dma((2,))] * 4,
+            *[dma((1,))] * 2,
+            *[dma((planes,))] * 12,
+        ],
+        compiler_params=pltpu.CompilerParams(
+            collective_id=0, has_side_effects=True, vmem_limit_bytes=52 << 20
+        ),
+    )(
+        query_states, key_states, value_states, sink_logits, segment_ids.reshape(1, -1), residual,
+        out_weight, norm_gain.reshape(1, -1), expert_ids, route_weights, gate_proj, up_proj, down_proj,
+    )
+
+
+def choose(mesh, *arrays):
+    query_states, key_states, residual, expert_ids = arrays[0], arrays[1], arrays[5], arrays[8]
+    planes, heads, pair = mesh.shape["seq"], mesh.shape["head"], mesh.shape["pair"]
+    rows = residual.shape[0]
+    experts = planes * heads // 2
+    sources = planes * heads * pair
+    capacity = min(rows, max(2, 3 * rows * expert_ids.shape[1] // (2 * experts)))
+    suits = (
+        pair == 1
+        and heads == 4
+        and planes > 1
+        and 3 * experts <= LANES
+        and key_states.shape[1] == 2 * HEAD_DIM
+        and 2 * HEAD_DIM == LANES
+        and query_states.shape[0] == 2 * WINDOW
+        and rows * 4 == query_states.shape[0]
+        and sources * rows <= 2 * sources * capacity
+    )
+    if suits:
+        return fused(planes, *arrays)
+    return per_device(*arrays)
+
+
 def solution(mesh):
     in_specs = (
         P(("group", "seq"), ("head", "pair")),
@@ -205,5 +641,5 @@
     )
     out_specs = P(("group", "seq", "head", "pair"), None)
     return jax.shard_map(
-        per_device, mesh=mesh, in_specs=in_specs, out_specs=out_specs, check_vma=False
-    )
+        functools.partial(choose, mesh), mesh=mesh, in_specs=in_specs, out_specs=out_specs, check_vma=False
+    )

time: 175 us -> 92.8 us (0.53); the launches traced: 172 us -> 92.4 us
  Pallas kernels: 0 us -> 84.5 us
  waiting for transfers between devices: 51.9 us -> 0 us
  blocking collectives: 34.1 us -> 0 us
  matrix products: 28.2 us -> 0 us
  between operations: 13.7 us -> 0.02 us
  starting transfers between devices: 13.6 us -> 0 us
  local copies, waits for them, and re-layouts: 19.8 us -> 7.91 us
  other arithmetic: 11.1 us -> 0 us
    pallas_call x0 -> x1, Pallas kernels: none -> 84.5 us  [fused(): pl.pallas_call(functools.partial(layer_kernel, planes, gate_proj.shape[0]...]
    all_to_all x1 -> x0, blocking collectives: 34.1 us -> none  [per_device(): lax.all_to_all(split_rows, ('seq', 'head'), split_axis=0, concat_axis=0,...]
    dot_general x9 -> x0, matrix products: 28.2 us -> none  [the longest x1 10.8 us: per_device(): jnp.dot(activated, down_local, preferred_element_type=jnp.float32)]
    all_to_all x1 -> x0, waiting for transfers between devices: 24.8 us -> none  [per_device(): lax.all_to_all(merged.astype(jnp.bfloat16), ('seq', 'head'), split_axis=0...]
    reduce_scatter x1 -> x0, waiting for transfers between devices: 21.3 us -> none  [per_device(): lax.psum_scatter(round_keep(jnp.dot(attended, out_weight, preferred_eleme...]
    ppermute x4 -> x0, starting transfers between devices: 9.04 us -> none  [the longest x2 8.41 us: passed_along(): return lax.ppermute(value, axis, pairs)]
    convert_element_type x4 -> x0, other arithmetic: 6.67 us -> none  [the longest x1 3.34 us: per_device(): merged.astype(jnp.bfloat16)]
    ppermute x4 -> x0, waiting for transfers between devices: 5.76 us -> none  [the longest x2 5.75 us: partner(): lax.ppermute(value, axis, [(i, i ^ 1 << distance) for i in range(lax.axis...]
  transfers between devices with their start and end apart: 6 -> 0, of which waited for: 4 -> 0; matrix products, arithmetic and copies ran while one was open for 6% -> 0% of each run, Pallas kernels for 0% -> 0%
where the time goes in v1:
time: 92.8 us; the launch traced here: 92.4 us
  Pallas kernels  84.5 us (91%)
  local copies, waits for them, and re-layouts  7.91 us (9%)
    pallas_call x1, Pallas kernels, fused(): pl.pallas_call(functools.partial(layer_kernel, planes, gate_proj.shape[0]...  84.5 us
    unnamed x15, local copies, waits for them, and re-layouts  7.21 us

profile of v1, /device:TPU:0, one launch (start us, length us, event | category | flops | bytes accessed | tf_op | source)
XLA Modules:
  0.0 92.4 jit_solution(18398729448144027915)
XLA Ops:
  0.0 0.7 reshape.7.gain_ref
  0.7 0.8 copy.14.ids_ref
  1.5 0.8 copy.15.rw_ref
  2.2 0.0 copy-start
  2.2 1.0 %copy-done = bf16[256,1024]{1,0:T(8,128)(2,1)S(1)} copy-done((bf16[256,1024]{1,0:T(8,128)(2,1)S(1)}, bf16[256,1024]{1,0:T(8,128)(2,1)}, u32[]{:S(2)}) %copy-start) | copy-done | bytes 524312
  3.3 0.0 copy-start.1
  3.3 0.9 %copy-done.1 = bf16[64,1536]{1,0:T(8,128)(2,1)S(1)} copy-done((bf16[64,1536]{1,0:T(8,128)(2,1)S(1)}, bf16[64,1536]{1,0:T(8,128)(2,1)}, u32[]{:S(2)}) %copy-start.1) | copy-done | bytes 196632
  4.2 0.0 copy-start.2
  4.2 0.8 copy-done.2
  5.1 0.0 copy-start.3
  5.1 0.8 copy-done.3
  5.9 0.0 copy-start.4
  5.9 0.7 copy-done.4
  6.6 0.0 copy-start.5
  6.6 0.7 copy-done.5
  7.2 84.5 %shard_map.127 = bf16[64,1536]{1,0:T(8,128)(2,1)S(1)} custom-call(bf16[256,1024]{1,0:T(8,128)(2,1)S(1)} %copy-done, bf16[256,128]{1,0:T(8,128)(2,1)S(1)} %copy-done.2, bf16[256,128]{1,0:T(8,128)(2,1)S(1)} %copy-done.3, f32[16]{0:T(128)S(1)} %copy-done.5, s32[1,1024]{1,0:T(1,128)S(1)} %bitcast.1, bf16[64,1536]{1,0:T(8,128)(2,1)S(1)} %copy-done.1, ...), custom_call_target="tpu_custom_call" | custom-call | tf_op jit(solution)/shard_map/pallas_call | solution.py:560
  91.8 0.7 copy.17
Async XLA Ops:
  2.2 1.0 %copy-start = (bf16[256,1024]{1,0:T(8,128)(2,1)S(1)}, bf16[256,1024]{1,0:T(8,128)(2,1)}, u32[]{:S(2)}) copy-start(bf16[256,1024]{1,0:T(8,128)(2,1)} %q_ref.1) | copy-start | bytes 1572868
  3.3 0.9 %copy-start.1 = (bf16[64,1536]{1,0:T(8,128)(2,1)S(1)}, bf16[64,1536]{1,0:T(8,128)(2,1)}, u32[]{:S(2)}) copy-start(bf16[64,1536]{1,0:T(8,128)(2,1)} %res_ref.1) | copy-start | bytes 589828
  4.2 0.8 copy-start.2
  5.1 0.8 copy-start.3
  5.9 0.7 copy-start.4
  6.6 0.7 copy-start.5

commit v2 on v1

--- a/solution.py
+++ b/solution.py
@@ -214,7 +214,7 @@
 
 
 def layer_kernel(
-    planes, experts,
+    planes, experts, split,
     q_ref, k_ref, v_ref, sink_ref, seg_ref, res_ref, wo_hbm, gain_ref, ids_ref, rw_ref,
     gate_hbm, up_hbm, down_hbm,
     out_ref,
@@ -406,22 +406,39 @@
     ]
     order = [pick([orders[own][step] for own in range(planes)], z) for step in range(planes)]
 
-    def gather_z(step):
-        there = order[step]
-        part = xbuf.at[z, mine]
-        return remote(part, part, gz_send.at[step], gz_recv.at[z], {"seq": there, "head": head})
-
-    def gather_z_got(step):
-        part = xbuf.at[order[step], mine]
-        return remote(part, part, gz_send.at[step], gz_recv.at[order[step]], {"seq": order[step], "head": head})
+    early, late = pl.ds(0, split), pl.ds(split, width + LANES - split)
+    parts = (0, 1) if split else (1,)
+
+    def along_z(p, toward, part):
+        block = xbuf.at[p, both_mine, early] if part == 0 else xbuf.at[p, mine, late]
+        beside = jnp.minimum(z + 1, planes - 1) if toward else jnp.maximum(z - 1, 0)
+        return remote(
+            block, block, gz_send.at[part, toward, p], gz_recv.at[part, p], {"seq": beside, "head": head}
+        )
+
+    def passing(step, act_on):
+        p = order[step]
+
+        @pl.when((p <= z) & (z < planes - 1))
+        def _():
+            act_on(p, 1)
+
+        @pl.when((p >= z) & (z > 0))
+        def _():
+            act_on(p, 0)
+
+    def arrived(step, part):
+        along_z(order[step], 0, part).wait_recv()
 
     def gather_x(step):
-        part = xbuf.at[order[step], mine]
-        return remote(part, part, gx_send.at[order[step]], gx_recv.at[order[step]], other_x)
+        p = order[step]
+        part = xbuf.at[p, mine] if step == 0 else xbuf.at[p, mine, late]
+        return remote(part, part, gx_send.at[p], gx_recv.at[p], other_x)
 
     def gather_x_got(step):
-        part = xbuf.at[order[step], its_x]
-        return remote(part, part, gx_send.at[order[step]], gx_recv.at[order[step]], other_x)
+        p = order[step]
+        part = xbuf.at[p, its_x] if step == 0 else xbuf.at[p, its_x, late]
+        return remote(part, part, gx_send.at[p], gx_recv.at[p], other_x)
 
     def gather_core(step):
         part = xbuf.at[order[step], both_mine]
@@ -475,9 +492,10 @@
             sum_z(step).start()
 
     gather_x(0).start()
-    for step in range(1, planes):
-        gather_z(step).start()
+    passing(0, lambda p, toward: along_z(p, toward, 1).start())
     gather_x_got(0).wait_recv()
+    if split:
+        passing(0, lambda p, toward: along_z(p, toward, 0).start())
     gather_core(0).start()
     for load in loads[1:]:
         load.wait()
@@ -487,8 +505,12 @@
     for step in range(planes):
         p = order[step]
         if step + 1 < planes:
-            gather_z_got(step + 1).wait_recv()
+            arrived(step + 1, 1)
             gather_x(step + 1).start()
+            passing(step + 1, lambda p, toward: along_z(p, toward, 1).start())
+            if split:
+                arrived(step + 1, 0)
+                passing(step + 1, lambda p, toward: along_z(p, toward, 0).start())
         gather_core_got(step).wait_recv()
 
         def hidden_units(n, _):
@@ -500,7 +522,7 @@
             return 0
 
         lax.fori_loop(0, ff // piece, hidden_units, 0)
-        if step >= 1:
+        if step >= 2:
             after_core(step - 1)
         if step + 1 < planes:
             gather_x_got(step + 1).wait_recv()
@@ -519,10 +541,14 @@
 
         lax.fori_loop(0, width // tile, outputs, 0)
         sum_core(step).start()
-        if step >= 1:
-            after_x(step - 1)
+        if step >= 3:
+            after_x(step - 2)
     after_core(planes - 1)
+    for step in range(max(1, planes - 2), planes - 1):
+        after_x(step)
+    after_core(0)
     after_x(planes - 1)
+    after_x(0)
     total = hidden[...]
     for step in range(1, planes):
         sum_z_got(step).wait_recv()
@@ -542,8 +568,9 @@
         sum_core(step).wait_send()
         sum_x(step).wait_send()
         if step:
-            gather_z(step).wait_send()
             sum_z(step).wait_send()
+        for part in parts:
+            passing(step, lambda p, toward, part=part: along_z(p, toward, part).wait_send())
 
 
 def fused(
@@ -554,11 +581,12 @@
     ff = gate_proj.shape[2]
     plane = 4 * rows
     tokens = query_states.shape[0]
+    split = (width + LANES) // 6 // LANES * LANES
     vmem, hbm = pl.BlockSpec(memory_space=pltpu.VMEM), pl.BlockSpec(memory_space=pl.ANY)
     smem = pl.BlockSpec(memory_space=pltpu.SMEM)
     dma = pltpu.SemaphoreType.DMA
     return pl.pallas_call(
-        functools.partial(layer_kernel, planes, gate_proj.shape[0] * planes * 4 // 2),
+        functools.partial(layer_kernel, planes, gate_proj.shape[0] * planes * 4 // 2, split),
         out_shape=jax.ShapeDtypeStruct((rows, width), BF16),
         in_specs=[vmem, vmem, vmem, smem, vmem, vmem, hbm, vmem, vmem, vmem, hbm, hbm, hbm],
         out_specs=vmem,
@@ -589,7 +617,9 @@
             dma((4,)),
             *[dma((2,))] * 4,
             *[dma((1,))] * 2,
-            *[dma((planes,))] * 12,
+            dma((2, 2, planes)),
+            dma((2, planes)),
+            *[dma((planes,))] * 10,
         ],
         compiler_params=pltpu.CompilerParams(
             collective_id=0, has_side_effects=True, vmem_limit_bytes=52 << 20

time: 92.8 us -> 83.6 us (0.901)
  Pallas kernels: 84.5 us -> 75.3 us
    pallas_call x1, Pallas kernels: 84.5 us -> 75.3 us  [fused(): pl.pallas_call(functools.partial(layer_kernel, planes, gate_proj.shape[0]...]
where the time goes in v2:
time: 83.6 us; the launch traced here: 83.2 us
  Pallas kernels  75.3 us (90%)
  local copies, waits for them, and re-layouts  7.91 us (9%)
    pallas_call x1, Pallas kernels, fused(): pl.pallas_call(functools.partial(layer_kernel, planes, gate_proj.shape[0]...  75.3 us
    unnamed x15, local copies, waits for them, and re-layouts  7.21 us

profile of v2, /device:TPU:0, one launch (start us, length us, event | category | flops | bytes accessed | tf_op | source)
XLA Modules:
  0.0 83.2 jit_solution(331837836695093750)
XLA Ops:
  0.0 0.7 reshape.7.gain_ref
  0.7 0.8 copy.14.ids_ref
  1.5 0.8 copy.15.rw_ref
  2.2 0.0 copy-start
  2.2 1.0 %copy-done = bf16[256,1024]{1,0:T(8,128)(2,1)S(1)} copy-done((bf16[256,1024]{1,0:T(8,128)(2,1)S(1)}, bf16[256,1024]{1,0:T(8,128)(2,1)}, u32[]{:S(2)}) %copy-start) | copy-done | bytes 524312
  3.3 0.0 copy-start.1
  3.3 0.9 %copy-done.1 = bf16[64,1536]{1,0:T(8,128)(2,1)S(1)} copy-done((bf16[64,1536]{1,0:T(8,128)(2,1)S(1)}, bf16[64,1536]{1,0:T(8,128)(2,1)}, u32[]{:S(2)}) %copy-start.1) | copy-done | bytes 196632
  4.2 0.0 copy-start.2
  4.2 0.8 %copy-done.2 = bf16[256,128]{1,0:T(8,128)(2,1)S(1)} copy-done((bf16[256,128]{1,0:T(8,128)(2,1)S(1)}, bf16[256,128]{1,0:T(8,128)(2,1)}, u32[]{:S(2)}) %copy-start.2) | copy-done | bytes 65560
  5.1 0.0 copy-start.3
  5.1 0.8 %copy-done.3 = bf16[256,128]{1,0:T(8,128)(2,1)S(1)} copy-done((bf16[256,128]{1,0:T(8,128)(2,1)S(1)}, bf16[256,128]{1,0:T(8,128)(2,1)}, u32[]{:S(2)}) %copy-start.3) | copy-done | bytes 65560
  5.9 0.0 copy-start.4
  5.9 0.7 copy-done.4
  6.6 0.0 copy-start.5
  6.6 0.7 copy-done.5
  7.2 75.3 %shard_map.127 = bf16[64,1536]{1,0:T(8,128)(2,1)S(1)} custom-call(bf16[256,1024]{1,0:T(8,128)(2,1)S(1)} %copy-done, bf16[256,128]{1,0:T(8,128)(2,1)S(1)} %copy-done.2, bf16[256,128]{1,0:T(8,128)(2,1)S(1)} %copy-done.3, f32[16]{0:T(128)S(1)} %copy-done.5, s32[1,1024]{1,0:T(1,128)S(1)} %bitcast.1, bf16[64,1536]{1,0:T(8,128)(2,1)S(1)} %copy-done.1, ...), custom_call_target="tpu_custom_call" | custom-call | tf_op jit(solution)/shard_map/pallas_call | solution.py:588
  82.5 0.7 copy.17
Async XLA Ops:
  2.2 1.0 %copy-start = (bf16[256,1024]{1,0:T(8,128)(2,1)S(1)}, bf16[256,1024]{1,0:T(8,128)(2,1)}, u32[]{:S(2)}) copy-start(bf16[256,1024]{1,0:T(8,128)(2,1)} %q_ref.1) | copy-start | bytes 1572868
  3.3 0.9 %copy-start.1 = (bf16[64,1536]{1,0:T(8,128)(2,1)S(1)}, bf16[64,1536]{1,0:T(8,128)(2,1)}, u32[]{:S(2)}) copy-start(bf16[64,1536]{1,0:T(8,128)(2,1)} %res_ref.1) | copy-start | bytes 589828
  4.2 0.8 %copy-start.2 = (bf16[256,128]{1,0:T(8,128)(2,1)S(1)}, bf16[256,128]{1,0:T(8,128)(2,1)}, u32[]{:S(2)}) copy-start(bf16[256,128]{1,0:T(8,128)(2,1)} %k_ref.1) | copy-start | bytes 196612
  5.1 0.8 %copy-start.3 = (bf16[256,128]{1,0:T(8,128)(2,1)S(1)}, bf16[256,128]{1,0:T(8,128)(2,1)}, u32[]{:S(2)}) copy-start(bf16[256,128]{1,0:T(8,128)(2,1)} %v_ref.1) | copy-start | bytes 196612
  5.9 0.7 copy-start.4
  6.6 0.7 copy-start.5
